TPU v7x, 32 devices: a whole 2x2x4 slice. The times are simulated.
32 devices in a mesh: replica: 4 (over y, x), space: 8 (over z, core).
Axes of the slice: x: 2, y: 2, z: 4, core: 2. Of those that a mesh axis runs over, the one named last changes fastest.
Arguments:
- inputs: bfloat16 [4, 64, 512, 256], P('replica', 'space'), may hold values from -6 to 6
- cotangent: bfloat16 [4, 64, 512, 256], P('replica', 'space'), may hold values from -6 to 6
- land_mask: int32 [64, 512], P('space'), may hold values 0 or 1
- weights: float32 [4, 2, 2304, 256], P('replica', None, 'space'), may hold values from -0.125 to 0.125
- momentum: float32 [4, 2, 2304, 256], P('replica', None, 'space'), may hold values from -6 to 6
- step: int32 [1], replicated, may hold values from 0 to 63
Outputs:
- grad_input: bfloat16 [4, 64, 512, 256], P('replica', 'space')
- new_weights: float32 [4, 2, 2304, 256], P('replica', None, 'space')
- new_momentum: float32 [4, 2, 2304, 256], P('replica', None, 'space')
All inputs are finite; a program needn't handle non-finite values. No bound on the sum of `land_mask` on one device may be relied on, other than what follows from the above.
Results may differ from a plain program's by a relative error of at most 0.012.
Values may be sent and summed in bfloat16 or wider, within the bound.
A program may use at most 256 MiB of HBM per device.

v0:
```python
from functools import partial
import math

import jax
import jax.numpy as jnp
from jax import lax
from jax.experimental import pallas as pl
from jax.experimental.pallas import tpu as pltpu
from jax.sharding import PartitionSpec as P

F32 = jnp.float32
BF16 = jnp.bfloat16
MESH = pl.DeviceIdType.MESH


def block_kernel(
    n, reps, levels, scale,
    coef, x_hbm, cot_hbm, mask_ref, w_ref, mom_ref,
    gi_hbm, nw_ref, nm_ref,
    xs, ms, ps, x_t, h_t, slope, cot, gi, kf, k_t, wb, mb, gb, sib, pair, far, gk, gw, gm, gg,
    loc_sem, halo_send, halo_recv, ag_send, ag_recv, agf_send, agf_recv,
    rs1_send, rs1_recv, rs2_send, rs2_recv, go_send, go_recv,
):
    rows, cols, chans = x_hbm.shape
    ext = rows + 2
    nz = n // 2
    sh = w_ref.shape[1]
    taps = 9
    q = lax.axis_index("replica")
    s = lax.axis_index("space")
    z = s // 2
    c = s % 2
    other = s + 1 - 2 * c

    def span(r, count=1):
        return pl.ds(pl.multiple_of(r * cols, cols), count * cols)

    def shard_rows(i):
        return pl.ds(pl.multiple_of(i * sh, 16), sh)

    def send(src, dst, ssem, rsem, rep, spc):
        return pltpu.make_async_remote_copy(
            src_ref=src, dst_ref=dst, send_sem=ssem, recv_sem=rsem,
            device_id=(rep, spc), device_id_type=MESH)

    started = []

    x_in = [pltpu.make_async_copy(x_hbm.at[r], xs.at[1, pl.ds((r + 1) * cols, cols)], loc_sem.at[r])
            for r in range(rows)]
    c_in = [pltpu.make_async_copy(cot_hbm.at[r], cot.at[pl.ds(r * cols, cols)], loc_sem.at[rows + r])
            for r in range(rows)]
    order = [0, rows - 1] + list(range(1, rows - 1))
    for r in order:
        x_in[r].start()
    for r in order:
        c_in[r].start()

    wb[...] = w_ref[...].astype(BF16)
    for k in range(2):
        kf[k, shard_rows(s), :] = w_ref[k].astype(BF16)

    barrier = pltpu.get_barrier_semaphore()
    for o in range(1, n):
        pl.semaphore_signal(barrier, inc=1, device_id=(q, (s + o) % n), device_id_type=MESH)
    for o in range(1, reps):
        pl.semaphore_signal(barrier, inc=1, device_id=((q + o) % reps, s), device_id_type=MESH)
    pl.semaphore_wait(barrier, n - 1 + reps - 1)

    def gather_start(k):
        out = []
        for o in range(1, nz):
            cp = send(kf.at[k, shard_rows(s)], kf.at[k, shard_rows(s)],
                      ag_send.at[k, o], ag_recv.at[k, o], q, ((z + o) % nz) * 2 + c)
            cp.start()
            out.append(cp)
        cp = send(kf.at[k, shard_rows(s)], kf.at[k, shard_rows(s)],
                  agf_send.at[k, 0], agf_recv.at[k, 0], q, other)
        cp.start()
        started.extend(out + [cp])
        return out, [cp]

    def gather_pass(k, far_copies, sib_copies):
        for o in range(1, nz):
            far_copies[o - 1].wait_recv()
            origin = ((z + nz - o) % nz) * 2 + c
            cp = send(kf.at[k, shard_rows(origin)], kf.at[k, shard_rows(origin)],
                      agf_send.at[k, o], agf_recv.at[k, o], q, other)
            cp.start()
            sib_copies.append(cp)
            started.append(cp)

    def gather_finish(sib_copies):
        for cp in sib_copies:
            cp.wait_recv()

    def halo(f, buf, go):
        lower = send(buf.at[1, span(1)], buf.at[1, span(ext - 1)],
                     halo_send.at[f, 0], halo_recv.at[f, 0], q, (s + n - 1) % n)
        upper = send(buf.at[1, span(rows)], buf.at[1, span(0)],
                     halo_send.at[f, 1], halo_recv.at[f, 1], q, (s + 1) % n)
        if go:
            @pl.when(s > 0)
            def _():
                lower.start()

            @pl.when(s < n - 1)
            def _():
                upper.start()
        else:
            @pl.when(s < n - 1)
            def _():
                lower.wait_recv()

            @pl.when(s > 0)
            def _():
                upper.wait_recv()

            @pl.when(s > 0)
            def _():
                lower.wait_send()

            @pl.when(s < n - 1)
            def _():
                upper.wait_send()

            @pl.when(s == 0)
            def _():
                buf[1, span(0), :] = jnp.zeros((cols, chans), BF16)

            @pl.when(s == n - 1)
            def _():
                buf[1, span(ext - 1), :] = jnp.zeros((cols, chans), BF16)

    def sides(buf, r, v):
        col = lax.broadcasted_iota(jnp.int32, (cols, chans), 0)
        buf[0, span(r), :] = jnp.where(col == 0, 0.0, pltpu.roll(v, 1, 0)).astype(BF16)
        buf[2, span(r), :] = jnp.where(col == cols - 1, 0.0, pltpu.roll(v, cols - 1, 0)).astype(BF16)

    far0, sib0 = gather_start(0)

    for r in order[:2]:
        x_in[r].wait()
    halo(0, xs, True)
    mask_t = jnp.transpose(mask_ref[...].astype(F32))

    def mask_row(r):
        c_in[r].wait()
        v = cot[pl.ds(r * cols, cols), :].astype(F32) * mask_t[:, r:r + 1]
        ms[1, pl.ds((r + 1) * cols, cols), :] = v.astype(BF16)
        sides(ms, r + 1, v)

    for r in order[:2]:
        mask_row(r)
    halo(1, ms, True)
    for r in order[2:]:
        x_in[r].wait()

    mb[...] = mom_ref[...].astype(BF16)
    for level in range(levels):
        to = (q + (1 << level)) % reps
        for j, (src, dst) in enumerate(((wb, gw), (mb, gm))):
            cp = send(src, dst.at[level], go_send.at[j, level], go_recv.at[j, level], to, s)
            cp.start()
            started.append(cp)
    early = started[-2 * levels:]

    for r in order[2:]:
        mask_row(r)

    def prep_x(r):
        v = xs[1, span(r), :]
        x_t[:, span(r)] = jnp.transpose(v)
        sides(xs, r, v.astype(F32))

    @pl.loop(1, rows + 1)
    def _(r):
        prep_x(r)

    halo(0, xs, False)
    prep_x(0)
    prep_x(ext - 1)
    halo(1, ms, False)
    sides(ms, 0, ms[1, span(0), :].astype(F32))
    sides(ms, ext - 1, ms[1, span(ext - 1), :].astype(F32))

    gather_pass(0, far0, sib0)
    far1, sib1 = gather_start(1)
    gather_finish(sib0)

    def conv(buf, ker, h, ahead):
        parts = []
        for i in range(3):
            for j in range(3):
                a, b = (i, j) if ahead else (2 - i, 2 - j)
                parts.append(buf[b, span(h + a), :])
        return jnp.dot(jnp.concatenate(parts, axis=1), ker[...], preferred_element_type=F32)

    def turn(k):
        @pl.loop(0, taps)
        def _(t):
            at = pl.ds(pl.multiple_of(t * chans, chans), chans)
            k_t[k, at, :] = jnp.transpose(kf[k, at, :])

    @pl.loop(0, rows)
    def _(h):
        pre = conv(xs, kf.at[0], h, True)
        sig = 1.0 / (1.0 + jnp.exp(-pre))
        slope[span(h), :] = sig * (1.0 + pre * (1.0 - sig))
        h_t[:, span(h)] = jnp.transpose((pre * sig).astype(BF16))

    def grads(k, lhs_of, rhs_of):
        @pl.loop(0, taps)
        def _(t):
            i = t // 3
            j = t % 3
            g = jnp.dot(lhs_of(i), rhs_of(i, j), preferred_element_type=F32)
            gb[k, pl.ds(pl.multiple_of(t * chans, chans), chans), :] = (g * scale).astype(BF16)

    def share_start(k):
        out = []
        for y in range(nz):
            cp = send(gb.at[k, shard_rows(2 * y + 1 - c)], sib.at[k, y],
                      rs1_send.at[k, y], rs1_recv.at[k, y], q, other)
            cp.start()
            out.append(cp)
        started.extend(out)
        return out

    def share_pass(k, copies):
        out = []
        for cp in copies:
            cp.wait_recv()
        for o in list(range(1, nz)) + [0]:
            y = (z + o) % nz
            both = gb[k, shard_rows(2 * y + c), :].astype(F32) + sib[k, y].astype(F32)
            pair[k, o] = both.astype(BF16)
            if o:
                cp = send(pair.at[k, o], far.at[k, o], rs2_send.at[k, o], rs2_recv.at[k, o],
                          q, y * 2 + c)
                cp.start()
                out.append(cp)
        started.extend(out)
        return out

    def share_finish(k, copies):
        total = pair[k, 0].astype(F32)
        for o in range(1, nz):
            copies[o - 1].wait_recv()
            total = total + far[k, o].astype(F32)
        gk[k] = total.astype(BF16)
        nm_ref[k] = total
        out = []
        for level in range(levels):
            cp = send(gk.at[k], gg.at[k, level], go_send.at[2 + k, level], go_recv.at[2 + k, level],
                      (q + (1 << level)) % reps, s)
            cp.start()
            out.append(cp)
        started.extend(out)
        return out

    def settle(k, copies):
        for cp in copies:
            cp.wait_recv()
        g_in = jnp.zeros((sh, chans), F32)
        m_in = jnp.zeros((sh, chans), F32)
        w_in = jnp.zeros((sh, chans), F32)
        for level in range(levels):
            g_in = g_in + coef[level] * gg[k, level].astype(F32)
            m_in = m_in + coef[level] * gm[level, k].astype(F32)
            w_in = w_in + coef[level] * gw[level, k].astype(F32)
        mixed = 0.5 * (0.9 * (mom_ref[k] + m_in) + nm_ref[k] + g_in)
        nm_ref[k] = mixed
        nw_ref[k] = 0.5 * (w_ref[k] + w_in) - 0.01 * mixed

    grads(1, lambda i: h_t[...], lambda i, j: ms[2 - j, span(2 - i, rows), :])
    share1 = share_start(1)
    gather_pass(1, far1, sib1)
    turn(0)
    gather_finish(sib1)
    turn(1)

    def back(h):
        v = conv(ms, k_t.at[1], h, False) * slope[span(h), :]
        ps[1, span(h + 1), :] = v.astype(BF16)
        sides(ps, h + 1, v)

    @pl.loop(0, 2)
    def _(t):
        back(t * (rows - 1))

    halo(2, ps, True)
    parts1 = share_pass(1, share1)

    @pl.loop(1, rows - 1)
    def _(h):
        back(h)

    grads(0, lambda i: x_t[:, span(i, rows)], lambda i, j: ps[2 - j, span(1, rows), :])
    share0 = share_start(0)

    def out_row(h):
        v = conv(ps, k_t.at[0], h, False) + ms[1, span(h + 1), :].astype(F32)
        gi[span(h), :] = v.astype(BF16)

    halo(2, ps, False)
    sides(ps, 0, ps[1, span(0), :].astype(F32))
    sides(ps, ext - 1, ps[1, span(ext - 1), :].astype(F32))
    parts0 = share_pass(0, share0)
    half = rows // 2

    @pl.loop(0, half)
    def _(h):
        out_row(h)

    last1 = share_finish(1, parts1)

    @pl.loop(half, rows)
    def _(h):
        out_row(h)

    stores = [pltpu.make_async_copy(gi.at[pl.ds(r * cols, cols)], gi_hbm.at[r], loc_sem.at[r])
              for r in range(rows)]
    for cp in stores:
        cp.start()
    for cp in early:
        cp.wait_recv()
    last0 = share_finish(0, parts0)
    settle(1, last1)
    settle(0, last0)
    for cp in stores:
        cp.wait()
    for cp in started:
        cp.wait_send()


def shards(inputs, cotangent, land_mask, weights, momentum, step):
    n = lax.axis_size("space")
    reps = lax.axis_size("replica")
    levels = reps.bit_length() - 1
    rows, cols, chans = inputs.shape[1:]
    sh = weights.shape[2]
    kc = sh * n
    ext = rows + 2
    nz = n // 2
    scale = 1.0 / math.sqrt(rows * n * cols)
    coef = (step[0] % levels == jnp.arange(levels)).astype(F32)
    vm = pltpu.VMEM
    sem = pltpu.SemaphoreType.DMA
    flops = 5 * 2 * rows * cols * kc * chans
    any_space = pl.BlockSpec(memory_space=pl.ANY)
    in_vmem = pl.BlockSpec(memory_space=pltpu.VMEM)
    gi, nw, nm = pl.pallas_call(
        partial(block_kernel, n, reps, levels, scale),
        out_shape=(
            jax.ShapeDtypeStruct((rows, cols, chans), BF16),
            jax.ShapeDtypeStruct((2, sh, chans), F32),
            jax.ShapeDtypeStruct((2, sh, chans), F32),
        ),
        in_specs=[pl.BlockSpec(memory_space=pltpu.SMEM), any_space, any_space,
                  in_vmem, in_vmem, in_vmem],
        out_specs=(any_space, in_vmem, in_vmem),
        scratch_shapes=[
            vm((3, ext * cols, chans), BF16),
            vm((3, ext * cols, chans), BF16),
            vm((3, ext * cols, chans), BF16),
            vm((chans, ext * cols), BF16),
            vm((chans, rows * cols), BF16),
            vm((rows * cols, chans), F32),
            vm((rows * cols, chans), BF16),
            vm((rows * cols, chans), BF16),
            vm((2, kc, chans), BF16),
            vm((2, kc, chans), BF16),
            vm((2, sh, chans), BF16),
            vm((2, sh, chans), BF16),
            vm((2, kc, chans), BF16),
            vm((2, nz, sh, chans), BF16),
            vm((2, nz, sh, chans), BF16),
            vm((2, nz, sh, chans), BF16),
            vm((2, sh, chans), BF16),
            vm((levels, 2, sh, chans), BF16),
            vm((levels, 2, sh, chans), BF16),
            vm((2, levels, sh, chans), BF16),
            sem((2 * rows,)),
            sem((3, 2)), sem((3, 2)),
            sem((2, nz)), sem((2, nz)), sem((2, nz)), sem((2, nz)),
            sem((2, nz)), sem((2, nz)), sem((2, nz)), sem((2, nz)),
            sem((4, levels)), sem((4, levels)),
        ],
        compiler_params=pltpu.CompilerParams(
            collective_id=0, has_side_effects=True, vmem_limit_bytes=60 * 1024 * 1024),
        cost_estimate=pl.CostEstimate(flops=flops, bytes_accessed=12 << 20, transcendentals=0),
    )(coef, inputs[0], cotangent[0], land_mask, weights[0], momentum[0])
    return gi[None], nw[None], nm[None]


def solution(mesh):
    in_specs = (
        P("replica", "space", None, None),
        P("replica", "space", None, None),
        P("space", None),
        P("replica", None, "space", None),
        P("replica", None, "space", None),
        P(),
    )
    out_specs = (
        P("replica", "space", None, None),
        P("replica", None, "space", None),
        P("replica", None, "space", None),
    )
    return jax.shard_map(shards, mesh=mesh, in_specs=in_specs, out_specs=out_specs, check_vma=False)
```

profile of v0, /device:TPU:8, one launch (start us, length us, event | category | flops | bytes accessed | tf_op | source)
XLA Modules:
  0.0 94.1 jit_solution(13036719366773796798)
XLA Ops:
  1.3 0.5 compare_convert_fusion.coef
  1.8 87.4 %shard_map.85 = (bf16[8,512,256]{2,1,0:T(8,128)(2,1)}, f32[2,288,256]{2,1,0:T(8,128)}, f32[2,288,256]{2,1,0:T(8,128)}) custom-call(f32[2]{0:T(128)} %compare_convert_fusion.coef, bf16[8,512,256]{2,1,0:T(8,128)(2,1)} %bitcast.14, bf16[8,512,256]{2,1,0:T(8,128)(2,1)} %bitcast.15, s32[8,512]{1,0:T(8,128)} %mask_ref.1, f32[2,288,256]{2,1,0:T(8,128)} %bitcast.16, ...), custom_call_target="tpu_custom_call" | custom-call | flops 24159191040 | bytes 12582912 | tf_op jit(solution)/shard_map/pallas_call | solution.py:352
  89.3 0.0 copy-start.1
  89.3 0.0 copy-start
  89.3 3.1 %copy.13 = bf16[1,8,512,256]{3,2,1,0:T(8,128)(2,1)} copy(bf16[1,8,512,256]{3,2,1,0:T(8,128)(2,1)} %bitcast.11) | data formatting | bytes 4194304
  92.4 0.0 copy-done.1
  92.4 0.8 copy.14
  93.2 0.0 copy-done
  93.2 0.8 copy.15
Async XLA Ops:
  89.3 3.2 %copy-start.1 = (f32[2,288,256]{2,1,0:T(8,128)S(1)}, f32[2,288,256]{2,1,0:T(8,128)}, u32[]{:S(2)}) copy-start(f32[2,288,256]{2,1,0:T(8,128)} %get-tuple-element.7) | copy-start | bytes 1769476
  89.3 4.0 %copy-start = (f32[2,288,256]{2,1,0:T(8,128)S(1)}, f32[2,288,256]{2,1,0:T(8,128)}, u32[]{:S(2)}) copy-start(f32[2,288,256]{2,1,0:T(8,128)} %get-tuple-element.8) | copy-start | bytes 1769476
where the time goes:
time: 95.9 us; the launch traced here: 94.1 us
  Pallas kernels  87.4 us (91%)
  local copies, waits for them, and re-layouts  4.78 us (5%)
  between operations  1.32 us (1%)
    pallas_call x1, Pallas kernels, shards(): pl.pallas_call(partial(block_kernel, n, reps, levels, scale), out_shape=(...  87.4 us
    unnamed x7, local copies, waits for them, and re-layouts  4.78 us

commit v1 on v0

--- a/solution.py
+++ b/solution.py
@@ -17,7 +17,7 @@
     n, reps, levels, scale,
     coef, x_hbm, cot_hbm, mask_ref, w_ref, mom_ref,
     gi_hbm, nw_ref, nm_ref,
-    xs, ms, ps, x_t, h_t, slope, cot, gi, kf, k_t, wb, mb, gb, sib, pair, far, gk, gw, gm, gg,
+    xs, ms, ps, x_t, m_t, hid, slope, cot, kf, k_t, wb, mb, gb, sib, pair, far, gk, gw, gm, gg,
     loc_sem, halo_send, halo_recv, ag_send, ag_recv, agf_send, agf_recv,
     rs1_send, rs1_recv, rs2_send, rs2_recv, go_send, go_recv,
 ):
@@ -133,8 +133,11 @@
 
     def sides(buf, r, v):
         col = lax.broadcasted_iota(jnp.int32, (cols, chans), 0)
-        buf[0, span(r), :] = jnp.where(col == 0, 0.0, pltpu.roll(v, 1, 0)).astype(BF16)
-        buf[2, span(r), :] = jnp.where(col == cols - 1, 0.0, pltpu.roll(v, cols - 1, 0)).astype(BF16)
+        left = jnp.where(col == 0, 0.0, pltpu.roll(v, 1, 0)).astype(BF16)
+        right = jnp.where(col == cols - 1, 0.0, pltpu.roll(v, cols - 1, 0)).astype(BF16)
+        buf[0, span(r), :] = left
+        buf[2, span(r), :] = right
+        return left, right
 
     far0, sib0 = gather_start(0)
 
@@ -147,7 +150,6 @@
         c_in[r].wait()
         v = cot[pl.ds(r * cols, cols), :].astype(F32) * mask_t[:, r:r + 1]
         ms[1, pl.ds((r + 1) * cols, cols), :] = v.astype(BF16)
-        sides(ms, r + 1, v)
 
     for r in order[:2]:
         mask_row(r)
@@ -167,24 +169,37 @@
     for r in order[2:]:
         mask_row(r)
 
-    def prep_x(r):
+    def prep_x(r, offsets):
         v = xs[1, span(r), :]
-        x_t[:, span(r)] = jnp.transpose(v)
+        flat = jnp.transpose(v)
+        for i in offsets:
+            x_t[pl.ds(i * chans, chans), span(r - i)] = flat
         sides(xs, r, v.astype(F32))
 
-    @pl.loop(1, rows + 1)
+    def prep_m(r):
+        v = ms[1, span(r), :]
+        left, right = sides(ms, r, v.astype(F32))
+        for i, part in enumerate((left, v, right)):
+            m_t[pl.ds(i * chans, chans), span(r)] = jnp.transpose(part)
+
+    @pl.loop(2, rows)
     def _(r):
-        prep_x(r)
-
+        prep_x(r, (0, 1, 2))
+
+    prep_x(1, (0, 1))
+    prep_x(rows, (1, 2))
     halo(0, xs, False)
-    prep_x(0)
-    prep_x(ext - 1)
-    halo(1, ms, False)
-    sides(ms, 0, ms[1, span(0), :].astype(F32))
-    sides(ms, ext - 1, ms[1, span(ext - 1), :].astype(F32))
+    prep_x(0, (0,))
+    prep_x(ext - 1, (2,))
 
     gather_pass(0, far0, sib0)
     far1, sib1 = gather_start(1)
+    halo(1, ms, False)
+
+    @pl.loop(0, ext)
+    def _(r):
+        prep_m(r)
+
     gather_finish(sib0)
 
     def conv(buf, ker, h, ahead):
@@ -192,7 +207,7 @@
         for i in range(3):
             for j in range(3):
                 a, b = (i, j) if ahead else (2 - i, 2 - j)
-                parts.append(buf[b, span(h + a), :])
+                parts.append(buf[b, span(h + a, 2), :])
         return jnp.dot(jnp.concatenate(parts, axis=1), ker[...], preferred_element_type=F32)
 
     def turn(k):
@@ -201,20 +216,15 @@
             at = pl.ds(pl.multiple_of(t * chans, chans), chans)
             k_t[k, at, :] = jnp.transpose(kf[k, at, :])
 
-    @pl.loop(0, rows)
+    @pl.loop(0, rows, step=2, unroll=2)
     def _(h):
         pre = conv(xs, kf.at[0], h, True)
         sig = 1.0 / (1.0 + jnp.exp(-pre))
-        slope[span(h), :] = sig * (1.0 + pre * (1.0 - sig))
-        h_t[:, span(h)] = jnp.transpose((pre * sig).astype(BF16))
-
-    def grads(k, lhs_of, rhs_of):
-        @pl.loop(0, taps)
-        def _(t):
-            i = t // 3
-            j = t % 3
-            g = jnp.dot(lhs_of(i), rhs_of(i, j), preferred_element_type=F32)
-            gb[k, pl.ds(pl.multiple_of(t * chans, chans), chans), :] = (g * scale).astype(BF16)
+        slope[span(h, 2), :] = sig * (1.0 + pre * (1.0 - sig))
+        hid[span(h, 2), :] = (pre * sig).astype(BF16)
+
+    def put_grad(k, tap, g):
+        gb[k, pl.ds(pl.multiple_of(tap * chans, chans), chans), :] = (g * scale).astype(BF16)
 
     def share_start(k):
         out = []
@@ -272,7 +282,12 @@
         nm_ref[k] = mixed
         nw_ref[k] = 0.5 * (w_ref[k] + w_in) - 0.01 * mixed
 
-    grads(1, lambda i: h_t[...], lambda i, j: ms[2 - j, span(2 - i, rows), :])
+    @pl.loop(0, 3)
+    def _(i):
+        g = jnp.dot(m_t[:, span(2 - i, rows)], hid[...], preferred_element_type=F32)
+        for j in range(3):
+            put_grad(1, 3 * i + j, jnp.transpose(g[(2 - j) * chans:(3 - j) * chans]))
+
     share1 = share_start(1)
     gather_pass(1, far1, sib1)
     turn(0)
@@ -280,27 +295,33 @@
     turn(1)
 
     def back(h):
-        v = conv(ms, k_t.at[1], h, False) * slope[span(h), :]
-        ps[1, span(h + 1), :] = v.astype(BF16)
-        sides(ps, h + 1, v)
-
-    @pl.loop(0, 2)
+        v = conv(ms, k_t.at[1], h, False) * slope[span(h, 2), :]
+        ps[1, span(h + 1, 2), :] = v.astype(BF16)
+        sides(ps, h + 1, v[:cols])
+        sides(ps, h + 2, v[cols:])
+
+    @pl.loop(0, 2, unroll=2)
     def _(t):
-        back(t * (rows - 1))
+        back(t * (rows - 2))
 
     halo(2, ps, True)
     parts1 = share_pass(1, share1)
 
-    @pl.loop(1, rows - 1)
+    @pl.loop(2, rows - 2, step=2, unroll=2)
     def _(h):
         back(h)
 
-    grads(0, lambda i: x_t[:, span(i, rows)], lambda i, j: ps[2 - j, span(1, rows), :])
+    @pl.loop(0, 3)
+    def _(j):
+        g = jnp.dot(x_t[...], ps[2 - j, span(1, rows), :], preferred_element_type=F32)
+        for i in range(3):
+            put_grad(0, 3 * i + j, g[i * chans:(i + 1) * chans])
+
     share0 = share_start(0)
 
     def out_row(h):
-        v = conv(ps, k_t.at[0], h, False) + ms[1, span(h + 1), :].astype(F32)
-        gi[span(h), :] = v.astype(BF16)
+        v = conv(ps, k_t.at[0], h, False) + ms[1, span(h + 1, 2), :].astype(F32)
+        cot[span(h, 2), :] = v.astype(BF16)
 
     halo(2, ps, False)
     sides(ps, 0, ps[1, span(0), :].astype(F32))
@@ -308,17 +329,17 @@
     parts0 = share_pass(0, share0)
     half = rows // 2
 
-    @pl.loop(0, half)
+    @pl.loop(0, half, step=2, unroll=2)
     def _(h):
         out_row(h)
 
     last1 = share_finish(1, parts1)
 
-    @pl.loop(half, rows)
+    @pl.loop(half, rows, step=2, unroll=2)
     def _(h):
         out_row(h)
 
-    stores = [pltpu.make_async_copy(gi.at[pl.ds(r * cols, cols)], gi_hbm.at[r], loc_sem.at[r])
+    stores = [pltpu.make_async_copy(cot.at[pl.ds(r * cols, cols)], gi_hbm.at[r], loc_sem.at[r])
               for r in range(rows)]
     for cp in stores:
         cp.start()
@@ -331,6 +352,17 @@
         cp.wait()
     for cp in started:
         cp.wait_send()
+
+
+def copy_kernel(gi, nw, nm, gi_out, nw_out, nm_out, done):
+    rows = gi.shape[0]
+    moves = [(gi.at[r], gi_out.at[r]) for r in range(rows)]
+    moves += [(nw.at[k], nw_out.at[k]) for k in range(2)] + [(nm.at[k], nm_out.at[k]) for k in range(2)]
+    copies = [pltpu.make_async_copy(a, b, done.at[i]) for i, (a, b) in enumerate(moves)]
+    for cp in copies:
+        cp.start()
+    for cp in copies:
+        cp.wait()
 
 
 def shards(inputs, cotangent, land_mask, weights, momentum, step):
@@ -363,10 +395,10 @@
             vm((3, ext * cols, chans), BF16),
             vm((3, ext * cols, chans), BF16),
             vm((3, ext * cols, chans), BF16),
-            vm((chans, ext * cols), BF16),
-            vm((chans, rows * cols), BF16),
+            vm((3 * chans, rows * cols), BF16),
+            vm((3 * chans, ext * cols), BF16),
+            vm((rows * cols, chans), BF16),
             vm((rows * cols, chans), F32),
-            vm((rows * cols, chans), BF16),
             vm((rows * cols, chans), BF16),
             vm((2, kc, chans), BF16),
             vm((2, kc, chans), BF16),
@@ -387,9 +419,16 @@
             sem((4, levels)), sem((4, levels)),
         ],
         compiler_params=pltpu.CompilerParams(
-            collective_id=0, has_side_effects=True, vmem_limit_bytes=60 * 1024 * 1024),
+            collective_id=0, has_side_effects=True, vmem_limit_bytes=63 * 1024 * 1024),
         cost_estimate=pl.CostEstimate(flops=flops, bytes_accessed=12 << 20, transcendentals=0),
     )(coef, inputs[0], cotangent[0], land_mask, weights[0], momentum[0])
+    gi, nw, nm = pl.pallas_call(
+        copy_kernel,
+        out_shape=tuple(jax.ShapeDtypeStruct(v.shape, v.dtype) for v in (gi, nw, nm)),
+        in_specs=[any_space] * 3,
+        out_specs=(any_space,) * 3,
+        scratch_shapes=[sem((rows + 4,))],
+    )(gi, nw, nm)
     return gi[None], nw[None], nm[None]
 
 

time: 95.9 us -> 192 us (2.00)
  Pallas kernels: 87.4 us -> 188 us
  local copies, waits for them, and re-layouts: 4.78 us -> 0 us
    pallas_call x0 -> x1, Pallas kernels: none -> 100 us  [shards(): pl.pallas_call(copy_kernel, out_shape=tuple((jax.ShapeDtypeStruct(v.shape...]
    unnamed x7 -> x0, local copies, waits for them, and re-layouts: 4.78 us -> none
where the time goes in v1:
time: 192 us; the launch traced here: 190 us
  Pallas kernels  188 us (98%)
    pallas_call x1, Pallas kernels, shards(): pl.pallas_call(copy_kernel, out_shape=tuple((jax.ShapeDtypeStruct(v.shape...  100 us
    pallas_call x1, Pallas kernels, shards(): pl.pallas_call(partial(block_kernel, n, reps, levels, scale), out_shape=(...  87.5 us

profile of v1, /device:TPU:8, one launch (start us, length us, event | category | flops | bytes accessed | tf_op | source)
XLA Modules:
  0.0 189.9 jit_solution(4514711853204906438)
XLA Ops:
  1.3 0.5 compare_convert_fusion.coef
  1.8 87.5 %shard_map.85 = (bf16[8,512,256]{2,1,0:T(8,128)(2,1)}, f32[2,288,256]{2,1,0:T(8,128)}, f32[2,288,256]{2,1,0:T(8,128)}) custom-call(f32[2]{0:T(128)} %compare_convert_fusion.coef, bf16[8,512,256]{2,1,0:T(8,128)(2,1)} %bitcast.11, bf16[8,512,256]{2,1,0:T(8,128)(2,1)} %bitcast.12, s32[8,512]{1,0:T(8,128)} %mask_ref.1, f32[2,288,256]{2,1,0:T(8,128)} %bitcast.14, ...), custom_call_target="tpu_custom_call" | custom-call | flops 24159191040 | bytes 12582912 | tf_op jit(solution)/shard_map/pallas_call | solution.py:384
  89.3 100.5 %shard_map.86 = (bf16[8,512,256]{2,1,0:T(8,128)(2,1)}, f32[2,288,256]{2,1,0:T(8,128)}, f32[2,288,256]{2,1,0:T(8,128)}) custom-call(bf16[8,512,256]{2,1,0:T(8,128)(2,1)} %get-tuple-element.9.gi, f32[2,288,256]{2,1,0:T(8,128)} %get-tuple-element.10.nw, f32[2,288,256]{2,1,0:T(8,128)} %get-tuple-element.11.nm), custom_call_target="tpu_custom_call" | custom-call | tf_op jit(solution)/shard_map/pallas_call | solution.py:425

commit v2 on v1

--- a/solution.py
+++ b/solution.py
@@ -66,32 +66,72 @@
         pl.semaphore_signal(barrier, inc=1, device_id=((q + o) % reps, s), device_id_type=MESH)
     pl.semaphore_wait(barrier, n - 1 + reps - 1)
 
+    def shard_send(k, chip, core, ssem, rsem, spc):
+        at = shard_rows(2 * chip + core)
+        return send(kf.at[k, at], kf.at[k, at], ssem, rsem, q, spc)
+
+    def may_send(d, hop):
+        if d == 0:
+            return (z + 1 >= hop) & (z + 1 < nz)
+        return (z + hop <= nz) & (z >= 1)
+
+    def has_come(d, hop):
+        return z >= hop if d == 0 else z + hop < nz
+
+    def hop_copy(k, d, hop):
+        chip = z + 1 - hop if d == 0 else z - 1 + hop
+        to = s + 2 if d == 0 else s - 2
+        return shard_send(k, chip, c, ag_send.at[k, d, hop], ag_recv.at[k, d, hop], to)
+
+    def come_chip(d, hop):
+        return z - hop if d == 0 else z + hop
+
+    def hop_start(k, d, hop):
+        @pl.when(may_send(d, hop))
+        def _():
+            hop_copy(k, d, hop).start()
+
+    def own_pass(k):
+        return shard_send(k, z, c, agf_send.at[k, 0, 0], agf_recv.at[k, 0, 0], other)
+
+    def come_pass(k, d, hop, core):
+        return shard_send(k, come_chip(d, hop), core, agf_send.at[k, d, hop],
+                          agf_recv.at[k, d, hop], other)
+
     def gather_start(k):
-        out = []
-        for o in range(1, nz):
-            cp = send(kf.at[k, shard_rows(s)], kf.at[k, shard_rows(s)],
-                      ag_send.at[k, o], ag_recv.at[k, o], q, ((z + o) % nz) * 2 + c)
-            cp.start()
-            out.append(cp)
-        cp = send(kf.at[k, shard_rows(s)], kf.at[k, shard_rows(s)],
-                  agf_send.at[k, 0], agf_recv.at[k, 0], q, other)
-        cp.start()
-        started.extend(out + [cp])
-        return out, [cp]
-
-    def gather_pass(k, far_copies, sib_copies):
-        for o in range(1, nz):
-            far_copies[o - 1].wait_recv()
-            origin = ((z + nz - o) % nz) * 2 + c
-            cp = send(kf.at[k, shard_rows(origin)], kf.at[k, shard_rows(origin)],
-                      agf_send.at[k, o], agf_recv.at[k, o], q, other)
-            cp.start()
-            sib_copies.append(cp)
-            started.append(cp)
-
-    def gather_finish(sib_copies):
-        for cp in sib_copies:
-            cp.wait_recv()
+        for d in range(2):
+            hop_start(k, d, 1)
+        own_pass(k).start()
+
+    def gather_hop(k, hop):
+        for d in range(2):
+            @pl.when(has_come(d, hop))
+            def _():
+                shard_send(k, come_chip(d, hop), c, ag_send.at[k, d, hop],
+                           ag_recv.at[k, d, hop], other).wait_recv()
+                if hop + 1 < nz:
+                    hop_start(k, d, hop + 1)
+                come_pass(k, d, hop, c).start()
+
+    def gather_finish(k):
+        own_pass(k).wait_recv()
+        for hop in range(1, nz):
+            for d in range(2):
+                @pl.when(has_come(d, hop))
+                def _():
+                    come_pass(k, d, hop, 1 - c).wait_recv()
+
+    def gather_close(k):
+        own_pass(k).wait_send()
+        for hop in range(1, nz):
+            for d in range(2):
+                @pl.when(may_send(d, hop))
+                def _():
+                    hop_copy(k, d, hop).wait_send()
+
+                @pl.when(has_come(d, hop))
+                def _():
+                    come_pass(k, d, hop, c).wait_send()
 
     def halo(f, buf, go):
         lower = send(buf.at[1, span(1)], buf.at[1, span(ext - 1)],
@@ -139,23 +179,14 @@
         buf[2, span(r), :] = right
         return left, right
 
-    far0, sib0 = gather_start(0)
-
-    for r in order[:2]:
-        x_in[r].wait()
-    halo(0, xs, True)
+    gather_start(0)
+
     mask_t = jnp.transpose(mask_ref[...].astype(F32))
 
     def mask_row(r):
         c_in[r].wait()
         v = cot[pl.ds(r * cols, cols), :].astype(F32) * mask_t[:, r:r + 1]
         ms[1, pl.ds((r + 1) * cols, cols), :] = v.astype(BF16)
-
-    for r in order[:2]:
-        mask_row(r)
-    halo(1, ms, True)
-    for r in order[2:]:
-        x_in[r].wait()
 
     mb[...] = mom_ref[...].astype(BF16)
     for level in range(levels):
@@ -166,8 +197,11 @@
             started.append(cp)
     early = started[-2 * levels:]
 
-    for r in order[2:]:
+    for r in order:
         mask_row(r)
+    gather_hop(0, 1)
+    for r in order:
+        x_in[r].wait()
 
     def prep_x(r, offsets):
         v = xs[1, span(r), :]
@@ -188,19 +222,19 @@
 
     prep_x(1, (0, 1))
     prep_x(rows, (1, 2))
-    halo(0, xs, False)
-    prep_x(0, (0,))
-    prep_x(ext - 1, (2,))
-
-    gather_pass(0, far0, sib0)
-    far1, sib1 = gather_start(1)
-    halo(1, ms, False)
-
-    @pl.loop(0, ext)
+    if nz > 2:
+        gather_hop(0, 2)
+
+    @pl.loop(1, rows + 1)
     def _(r):
         prep_m(r)
 
-    gather_finish(sib0)
+    for hop in range(3, nz):
+        gather_hop(0, hop)
+    halo(0, xs, True)
+    halo(1, ms, True)
+    gather_start(1)
+    gather_finish(0)
 
     def conv(buf, ker, h, ahead):
         parts = []
@@ -216,47 +250,71 @@
             at = pl.ds(pl.multiple_of(t * chans, chans), chans)
             k_t[k, at, :] = jnp.transpose(kf[k, at, :])
 
-    @pl.loop(0, rows, step=2, unroll=2)
-    def _(h):
+    def ahead(h):
         pre = conv(xs, kf.at[0], h, True)
         sig = 1.0 / (1.0 + jnp.exp(-pre))
         slope[span(h, 2), :] = sig * (1.0 + pre * (1.0 - sig))
         hid[span(h, 2), :] = (pre * sig).astype(BF16)
 
+    @pl.loop(2, rows - 2, step=2, unroll=2)
+    def _(h):
+        ahead(h)
+
+    gather_hop(1, 1)
+    halo(0, xs, False)
+    prep_x(0, (0,))
+    prep_x(ext - 1, (2,))
+
+    @pl.loop(0, 2, unroll=2)
+    def _(t):
+        ahead(t * (rows - 2))
+
+    if nz > 2:
+        gather_hop(1, 2)
+    halo(1, ms, False)
+    prep_m(0)
+    prep_m(ext - 1)
+
     def put_grad(k, tap, g):
         gb[k, pl.ds(pl.multiple_of(tap * chans, chans), chans), :] = (g * scale).astype(BF16)
 
-    def share_start(k):
-        out = []
-        for y in range(nz):
-            cp = send(gb.at[k, shard_rows(2 * y + 1 - c)], sib.at[k, y],
-                      rs1_send.at[k, y], rs1_recv.at[k, y], q, other)
+    ends_first = sorted(range(nz), key=lambda y: (min(y, nz - 1 - y), y))
+
+    def share_copy(k, y):
+        return send(gb.at[k, shard_rows(2 * y + 1 - c)], sib.at[k, y],
+                    rs1_send.at[k, y], rs1_recv.at[k, y], q, other)
+
+    def share_start(k, chips):
+        for y in chips:
+            cp = share_copy(k, y)
             cp.start()
-            out.append(cp)
-        started.extend(out)
-        return out
-
-    def share_pass(k, copies):
-        out = []
-        for cp in copies:
-            cp.wait_recv()
-        for o in list(range(1, nz)) + [0]:
+            started.append(cp)
+
+    def far_copy(k, y):
+        return send(pair.at[k, y], far.at[k, z], rs2_send.at[k, y], rs2_recv.at[k, z],
+                    q, y * 2 + c)
+
+    def share_pass(k, chips):
+        for y in chips:
+            share_copy(k, y).wait_recv()
+            both = gb[k, shard_rows(2 * y + c), :].astype(F32) + sib[k, y].astype(F32)
+            pair[k, y] = both.astype(BF16)
+
+            @pl.when(z != y)
+            def _():
+                far_copy(k, y).start()
+
+    def share_close(k):
+        for o in range(1, nz):
+            far_copy(k, (z + o) % nz).wait_send()
+
+    def share_finish(k):
+        total = pair[k, z].astype(F32)
+        for o in range(1, nz):
             y = (z + o) % nz
-            both = gb[k, shard_rows(2 * y + c), :].astype(F32) + sib[k, y].astype(F32)
-            pair[k, o] = both.astype(BF16)
-            if o:
-                cp = send(pair.at[k, o], far.at[k, o], rs2_send.at[k, o], rs2_recv.at[k, o],
-                          q, y * 2 + c)
-                cp.start()
-                out.append(cp)
-        started.extend(out)
-        return out
-
-    def share_finish(k, copies):
-        total = pair[k, 0].astype(F32)
-        for o in range(1, nz):
-            copies[o - 1].wait_recv()
-            total = total + far[k, o].astype(F32)
+            send(pair.at[k, y], far.at[k, y], rs2_send.at[k, y], rs2_recv.at[k, y],
+                 q, y * 2 + c).wait_recv()
+            total = total + far[k, y].astype(F32)
         gk[k] = total.astype(BF16)
         nm_ref[k] = total
         out = []
@@ -282,16 +340,17 @@
         nm_ref[k] = mixed
         nw_ref[k] = 0.5 * (w_ref[k] + w_in) - 0.01 * mixed
 
-    @pl.loop(0, 3)
-    def _(i):
-        g = jnp.dot(m_t[:, span(2 - i, rows)], hid[...], preferred_element_type=F32)
+    for i in (1, 0, 2):
+        g = jnp.dot(m_t[:, (2 - i) * cols:(2 - i + rows) * cols], hid[...],
+                    preferred_element_type=F32)
         for j in range(3):
             put_grad(1, 3 * i + j, jnp.transpose(g[(2 - j) * chans:(3 - j) * chans]))
-
-    share1 = share_start(1)
-    gather_pass(1, far1, sib1)
-    turn(0)
-    gather_finish(sib1)
+        if i == 1:
+            for hop in range(3, nz):
+                gather_hop(1, hop)
+
+    share_start(1, ends_first)
+    gather_finish(1)
     turn(1)
 
     def back(h):
@@ -305,19 +364,28 @@
         back(t * (rows - 2))
 
     halo(2, ps, True)
-    parts1 = share_pass(1, share1)
+    share_pass(1, ends_first)
 
     @pl.loop(2, rows - 2, step=2, unroll=2)
     def _(h):
         back(h)
 
-    @pl.loop(0, 3)
-    def _(j):
-        g = jnp.dot(x_t[...], ps[2 - j, span(1, rows), :], preferred_element_type=F32)
-        for i in range(3):
-            put_grad(0, 3 * i + j, g[i * chans:(i + 1) * chans])
-
-    share0 = share_start(0)
+    done, sent, passed = set(), [], []
+    for i in (0, 2, 1):
+        for j in range(3):
+            put_grad(0, 3 * i + j, jnp.dot(
+                x_t[i * chans:(i + 1) * chans, :], ps[2 - j, cols:(rows + 1) * cols, :],
+                preferred_element_type=F32))
+            done.add(3 * i + j)
+        share_pass(0, [y for y in sent if y not in passed])
+        passed = list(sent)
+        ready = [y for y in ends_first if y not in sent and all(
+            tap in done for tap in range(2 * y * sh // chans, (2 * (y + 1) * sh - 1) // chans + 1))]
+        share_start(0, ready)
+        sent = sent + ready
+
+    turn(0)
+    share_pass(0, [y for y in sent if y not in passed])
 
     def out_row(h):
         v = conv(ps, k_t.at[0], h, False) + ms[1, span(h + 1, 2), :].astype(F32)
@@ -326,14 +394,13 @@
     halo(2, ps, False)
     sides(ps, 0, ps[1, span(0), :].astype(F32))
     sides(ps, ext - 1, ps[1, span(ext - 1), :].astype(F32))
-    parts0 = share_pass(0, share0)
     half = rows // 2
 
     @pl.loop(0, half, step=2, unroll=2)
     def _(h):
         out_row(h)
 
-    last1 = share_finish(1, parts1)
+    last1 = share_finish(1)
 
     @pl.loop(half, rows, step=2, unroll=2)
     def _(h):
@@ -345,23 +412,31 @@
         cp.start()
     for cp in early:
         cp.wait_recv()
-    last0 = share_finish(0, parts0)
+    last0 = share_finish(0)
     settle(1, last1)
     settle(0, last0)
     for cp in stores:
         cp.wait()
     for cp in started:
         cp.wait_send()
-
-
-def copy_kernel(gi, nw, nm, gi_out, nw_out, nm_out, done):
+    for k in range(2):
+        gather_close(k)
+        share_close(k)
+
+
+def copy_kernel(gi, nw, nm, gi_out, nw_out, nm_out, gi_at, w_at, m_at, came, left):
     rows = gi.shape[0]
-    moves = [(gi.at[r], gi_out.at[r]) for r in range(rows)]
-    moves += [(nw.at[k], nw_out.at[k]) for k in range(2)] + [(nm.at[k], nm_out.at[k]) for k in range(2)]
-    copies = [pltpu.make_async_copy(a, b, done.at[i]) for i, (a, b) in enumerate(moves)]
-    for cp in copies:
+    moves = [(gi.at[r], gi_at.at[r], gi_out.at[r]) for r in range(rows)]
+    moves += [(nw.at[k], w_at.at[k], nw_out.at[k]) for k in range(2)]
+    moves += [(nm.at[k], m_at.at[k], nm_out.at[k]) for k in range(2)]
+    loads = [pltpu.make_async_copy(a, b, came.at[i]) for i, (a, b, _) in enumerate(moves)]
+    stores = [pltpu.make_async_copy(b, d, left.at[i]) for i, (_, b, d) in enumerate(moves)]
+    for cp in loads:
         cp.start()
-    for cp in copies:
+    for a, b in zip(loads, stores):
+        a.wait()
+        b.start()
+    for cp in stores:
         cp.wait()
 
 
@@ -414,7 +489,7 @@
             vm((2, levels, sh, chans), BF16),
             sem((2 * rows,)),
             sem((3, 2)), sem((3, 2)),
-            sem((2, nz)), sem((2, nz)), sem((2, nz)), sem((2, nz)),
+            sem((2, 2, nz)), sem((2, 2, nz)), sem((2, 2, nz)), sem((2, 2, nz)),
             sem((2, nz)), sem((2, nz)), sem((2, nz)), sem((2, nz)),
             sem((4, levels)), sem((4, levels)),
         ],
@@ -427,7 +502,9 @@
         out_shape=tuple(jax.ShapeDtypeStruct(v.shape, v.dtype) for v in (gi, nw, nm)),
         in_specs=[any_space] * 3,
         out_specs=(any_space,) * 3,
-        scratch_shapes=[sem((rows + 4,))],
+        scratch_shapes=[vm(gi.shape, BF16), vm(nw.shape, F32), vm(nm.shape, F32),
+                        sem((rows + 4,)), sem((rows + 4,))],
+        compiler_params=pltpu.CompilerParams(vmem_limit_bytes=16 * 1024 * 1024),
     )(gi, nw, nm)
     return gi[None], nw[None], nm[None]
 

time: 192 us -> 92.6 us (0.48)
  Pallas kernels: 188 us -> 86.6 us
  local copies, waits for them, and re-layouts: 0 us -> 3.71 us
    pallas_call x1, Pallas kernels: 100 us -> 2.29 us  [shards(): pl.pallas_call(copy_kernel, out_shape=tuple((jax.ShapeDtypeStruct(v.shape...]
    unnamed x0 -> x6, local copies, waits for them, and re-layouts: none -> 3.71 us
    pallas_call x1, Pallas kernels: 87.5 us -> 84.3 us  [shards(): pl.pallas_call(partial(block_kernel, n, reps, levels, scale), out_shape=(...]
where the time goes in v2:
time: 92.6 us; the launch traced here: 92.4 us
  Pallas kernels  86.6 us (94%)
  local copies, waits for them, and re-layouts  3.71 us (4%)
  between operations  1.49 us (2%)
    pallas_call x1, Pallas kernels, shards(): pl.pallas_call(partial(block_kernel, n, reps, levels, scale), out_shape=(...  84.3 us
    unnamed x6, local copies, waits for them, and re-layouts  3.71 us
    pallas_call x1, Pallas kernels, shards(): pl.pallas_call(copy_kernel, out_shape=tuple((jax.ShapeDtypeStruct(v.shape...  2.29 us

profile of v2, /device:TPU:8, one launch (start us, length us, event | category | flops | bytes accessed | tf_op | source)
XLA Modules:
  0.0 92.4 jit_solution(13799006593506903729)
XLA Ops:
  1.3 0.5 compare_convert_fusion.coef
  1.8 84.3 %shard_map.85 = (bf16[8,512,256]{2,1,0:T(8,128)(2,1)}, f32[2,288,256]{2,1,0:T(8,128)}, f32[2,288,256]{2,1,0:T(8,128)}) custom-call(f32[2]{0:T(128)} %compare_convert_fusion.coef, bf16[8,512,256]{2,1,0:T(8,128)(2,1)} %bitcast.11, bf16[8,512,256]{2,1,0:T(8,128)(2,1)} %bitcast.12, s32[8,512]{1,0:T(8,128)} %mask_ref.1, f32[2,288,256]{2,1,0:T(8,128)} %bitcast.14, ...), custom_call_target="tpu_custom_call" | custom-call | flops 24159191040 | bytes 12582912 | tf_op jit(solution)/shard_map/pallas_call | solution.py:459
  86.2 0.0 copy-start
  86.2 1.6 %copy-done = bf16[8,512,256]{2,1,0:T(8,128)(2,1)S(1)} copy-done((bf16[8,512,256]{2,1,0:T(8,128)(2,1)S(1)}, bf16[8,512,256]{2,1,0:T(8,128)(2,1)}, u32[]{:S(2)}) %copy-start) | copy-done | bytes 2097176
  87.8 0.0 copy-start.1
  87.8 1.1 %copy-done.1 = f32[2,288,256]{2,1,0:T(8,128)S(1)} copy-done((f32[2,288,256]{2,1,0:T(8,128)S(1)}, f32[2,288,256]{2,1,0:T(8,128)}, u32[]{:S(2)}) %copy-start.1) | copy-done | bytes 589848
  88.8 0.0 copy-start.2
  88.8 1.1 %copy-done.2 = f32[2,288,256]{2,1,0:T(8,128)S(1)} copy-done((f32[2,288,256]{2,1,0:T(8,128)S(1)}, f32[2,288,256]{2,1,0:T(8,128)}, u32[]{:S(2)}) %copy-start.2) | copy-done | bytes 589848
  89.9 2.3 %shard_map.86 = (bf16[8,512,256]{2,1,0:T(8,128)(2,1)}, f32[2,288,256]{2,1,0:T(8,128)}, f32[2,288,256]{2,1,0:T(8,128)}) custom-call(bf16[8,512,256]{2,1,0:T(8,128)(2,1)S(1)} %copy-done, f32[2,288,256]{2,1,0:T(8,128)S(1)} %copy-done.1, f32[2,288,256]{2,1,0:T(8,128)S(1)} %copy-done.2), custom_call_target="tpu_custom_call" | custom-call | tf_op jit(solution)/shard_map/pallas_call | solution.py:500
Async XLA Ops:
  86.2 1.6 %copy-start = (bf16[8,512,256]{2,1,0:T(8,128)(2,1)S(1)}, bf16[8,512,256]{2,1,0:T(8,128)(2,1)}, u32[]{:S(2)}) copy-start(bf16[8,512,256]{2,1,0:T(8,128)(2,1)} %get-tuple-element.9.gi) | copy-start | bytes 6291460
  87.8 1.1 %copy-start.1 = (f32[2,288,256]{2,1,0:T(8,128)S(1)}, f32[2,288,256]{2,1,0:T(8,128)}, u32[]{:S(2)}) copy-start(f32[2,288,256]{2,1,0:T(8,128)} %get-tuple-element.10.nw) | copy-start | bytes 1769476
  88.8 1.1 %copy-start.2 = (f32[2,288,256]{2,1,0:T(8,128)S(1)}, f32[2,288,256]{2,1,0:T(8,128)}, u32[]{:S(2)}) copy-start(f32[2,288,256]{2,1,0:T(8,128)} %get-tuple-element.11.nm) | copy-start | bytes 1769476

commit v3 on v2

--- a/solution.py
+++ b/solution.py
@@ -17,7 +17,7 @@
     n, reps, levels, scale,
     coef, x_hbm, cot_hbm, mask_ref, w_ref, mom_ref,
     gi_hbm, nw_ref, nm_ref,
-    xs, ms, ps, x_t, m_t, hid, slope, cot, kf, k_t, wb, mb, gb, sib, pair, far, gk, gw, gm, gg,
+    xs, ms, ps, x_t, h_t, slope, cot, kf, k_t, wb, mb, gb, sib, pair, far, gk, gw, gm, gg,
     loc_sem, halo_send, halo_recv, ag_send, ag_recv, agf_send, agf_recv,
     rs1_send, rs1_recv, rs2_send, rs2_recv, go_send, go_recv,
 ):
@@ -203,25 +203,23 @@
     for r in order:
         x_in[r].wait()
 
-    def prep_x(r, offsets):
+    def prep_x(r):
         v = xs[1, span(r), :]
-        flat = jnp.transpose(v)
-        for i in offsets:
-            x_t[pl.ds(i * chans, chans), span(r - i)] = flat
+        x_t[:, span(r)] = jnp.transpose(v)
         sides(xs, r, v.astype(F32))
 
     def prep_m(r):
-        v = ms[1, span(r), :]
-        left, right = sides(ms, r, v.astype(F32))
-        for i, part in enumerate((left, v, right)):
-            m_t[pl.ds(i * chans, chans), span(r)] = jnp.transpose(part)
-
-    @pl.loop(2, rows)
+        sides(ms, r, ms[1, span(r), :].astype(F32))
+
+    def edges(prep):
+        @pl.loop(0, 2)
+        def _(e):
+            prep(e * (ext - 1))
+
+    @pl.loop(1, rows + 1)
     def _(r):
-        prep_x(r, (0, 1, 2))
-
-    prep_x(1, (0, 1))
-    prep_x(rows, (1, 2))
+        prep_x(r)
+
     if nz > 2:
         gather_hop(0, 2)
 
@@ -250,30 +248,26 @@
             at = pl.ds(pl.multiple_of(t * chans, chans), chans)
             k_t[k, at, :] = jnp.transpose(kf[k, at, :])
 
-    def ahead(h):
+    half = rows // 2
+
+    @pl.loop(0, half)
+    def _(e):
+        @pl.when(e == half - 2)
+        def _():
+            gather_hop(1, 1)
+            halo(0, xs, False)
+            edges(prep_x)
+
+        h = (2 * e + 2) % rows
         pre = conv(xs, kf.at[0], h, True)
-        sig = 1.0 / (1.0 + jnp.exp(-pre))
+        sig = 0.5 * jnp.tanh(0.5 * pre) + 0.5
         slope[span(h, 2), :] = sig * (1.0 + pre * (1.0 - sig))
-        hid[span(h, 2), :] = (pre * sig).astype(BF16)
-
-    @pl.loop(2, rows - 2, step=2, unroll=2)
-    def _(h):
-        ahead(h)
-
-    gather_hop(1, 1)
-    halo(0, xs, False)
-    prep_x(0, (0,))
-    prep_x(ext - 1, (2,))
-
-    @pl.loop(0, 2, unroll=2)
-    def _(t):
-        ahead(t * (rows - 2))
+        h_t[:, span(h, 2)] = jnp.transpose((pre * sig).astype(BF16))
 
     if nz > 2:
         gather_hop(1, 2)
     halo(1, ms, False)
-    prep_m(0)
-    prep_m(ext - 1)
+    edges(prep_m)
 
     def put_grad(k, tap, g):
         gb[k, pl.ds(pl.multiple_of(tap * chans, chans), chans), :] = (g * scale).astype(BF16)
@@ -286,9 +280,7 @@
 
     def share_start(k, chips):
         for y in chips:
-            cp = share_copy(k, y)
-            cp.start()
-            started.append(cp)
+            share_copy(k, y).start()
 
     def far_copy(k, y):
         return send(pair.at[k, y], far.at[k, z], rs2_send.at[k, y], rs2_recv.at[k, z],
@@ -305,8 +297,14 @@
                 far_copy(k, y).start()
 
     def share_close(k):
+        for y in range(nz):
+            share_copy(k, y).wait_send()
         for o in range(1, nz):
             far_copy(k, (z + o) % nz).wait_send()
+
+    def gossip_copy(k, level):
+        return send(gk.at[k], gg.at[k, level], go_send.at[2 + k, level], go_recv.at[2 + k, level],
+                    (q + (1 << level)) % reps, s)
 
     def share_finish(k):
         total = pair[k, z].astype(F32)
@@ -317,18 +315,12 @@
             total = total + far[k, y].astype(F32)
         gk[k] = total.astype(BF16)
         nm_ref[k] = total
-        out = []
         for level in range(levels):
-            cp = send(gk.at[k], gg.at[k, level], go_send.at[2 + k, level], go_recv.at[2 + k, level],
-                      (q + (1 << level)) % reps, s)
-            cp.start()
-            out.append(cp)
-        started.extend(out)
-        return out
-
-    def settle(k, copies):
-        for cp in copies:
-            cp.wait_recv()
+            gossip_copy(k, level).start()
+
+    def settle(k):
+        for level in range(levels):
+            gossip_copy(k, level).wait_recv()
         g_in = jnp.zeros((sh, chans), F32)
         m_in = jnp.zeros((sh, chans), F32)
         w_in = jnp.zeros((sh, chans), F32)
@@ -340,71 +332,73 @@
         nm_ref[k] = mixed
         nw_ref[k] = 0.5 * (w_ref[k] + w_in) - 0.01 * mixed
 
-    for i in (1, 0, 2):
-        g = jnp.dot(m_t[:, (2 - i) * cols:(2 - i + rows) * cols], hid[...],
-                    preferred_element_type=F32)
-        for j in range(3):
-            put_grad(1, 3 * i + j, jnp.transpose(g[(2 - j) * chans:(3 - j) * chans]))
-        if i == 1:
+    @pl.loop(0, taps)
+    def _(tap):
+        @pl.when(tap == 3)
+        def _():
             for hop in range(3, nz):
                 gather_hop(1, hop)
+
+        put_grad(1, tap, jnp.dot(h_t[...], ms[2 - tap % 3, span(2 - tap // 3, rows), :],
+                                 preferred_element_type=F32))
 
     share_start(1, ends_first)
     gather_finish(1)
     turn(1)
 
-    def back(h):
+    @pl.loop(0, half)
+    def _(e):
+        h = (2 * e + rows - 2) % rows
         v = conv(ms, k_t.at[1], h, False) * slope[span(h, 2), :]
         ps[1, span(h + 1, 2), :] = v.astype(BF16)
         sides(ps, h + 1, v[:cols])
         sides(ps, h + 2, v[cols:])
 
-    @pl.loop(0, 2, unroll=2)
-    def _(t):
-        back(t * (rows - 2))
-
-    halo(2, ps, True)
-    share_pass(1, ends_first)
-
-    @pl.loop(2, rows - 2, step=2, unroll=2)
-    def _(h):
-        back(h)
-
-    done, sent, passed = set(), [], []
+        @pl.when(e == 1)
+        def _():
+            halo(2, ps, True)
+            share_pass(1, ends_first)
+
+    done, sent, plan = set(), [], []
     for i in (0, 2, 1):
-        for j in range(3):
-            put_grad(0, 3 * i + j, jnp.dot(
-                x_t[i * chans:(i + 1) * chans, :], ps[2 - j, cols:(rows + 1) * cols, :],
-                preferred_element_type=F32))
-            done.add(3 * i + j)
-        share_pass(0, [y for y in sent if y not in passed])
-        passed = list(sent)
+        done.update((3 * i, 3 * i + 1, 3 * i + 2))
         ready = [y for y in ends_first if y not in sent and all(
             tap in done for tap in range(2 * y * sh // chans, (2 * (y + 1) * sh - 1) // chans + 1))]
-        share_start(0, ready)
+        plan.append(ready)
         sent = sent + ready
 
+    @pl.loop(0, taps)
+    def _(e):
+        @pl.when(e == 3)
+        def _():
+            share_start(0, plan[0])
+
+        @pl.when(e == 6)
+        def _():
+            share_start(0, plan[1])
+            share_pass(0, plan[0])
+
+        i = (2 * (e // 3)) % 3
+        j = e % 3
+        put_grad(0, 3 * i + j, jnp.dot(x_t[:, span(i, rows)], ps[2 - j, span(1, rows), :],
+                                       preferred_element_type=F32))
+
+    share_start(0, plan[2])
+    share_pass(0, plan[1])
     turn(0)
-    share_pass(0, [y for y in sent if y not in passed])
-
-    def out_row(h):
+    share_pass(0, plan[2])
+
+    @pl.loop(0, half)
+    def _(e):
+        @pl.when(e == half - 2)
+        def _():
+            halo(2, ps, False)
+            edges(lambda r: sides(ps, r, ps[1, span(r), :].astype(F32)))
+            share_finish(1)
+
+        h = (2 * e + 2) % rows
         v = conv(ps, k_t.at[0], h, False) + ms[1, span(h + 1, 2), :].astype(F32)
         cot[span(h, 2), :] = v.astype(BF16)
-
-    halo(2, ps, False)
-    sides(ps, 0, ps[1, span(0), :].astype(F32))
-    sides(ps, ext - 1, ps[1, span(ext - 1), :].astype(F32))
-    half = rows // 2
-
-    @pl.loop(0, half, step=2, unroll=2)
-    def _(h):
-        out_row(h)
-
-    last1 = share_finish(1)
-
-    @pl.loop(half, rows, step=2, unroll=2)
-    def _(h):
-        out_row(h)
 
     stores = [pltpu.make_async_copy(cot.at[pl.ds(r * cols, cols)], gi_hbm.at[r], loc_sem.at[r])
               for r in range(rows)]
@@ -412,9 +406,9 @@
         cp.start()
     for cp in early:
         cp.wait_recv()
-    last0 = share_finish(0)
-    settle(1, last1)
-    settle(0, last0)
+    share_finish(0)
+    settle(1)
+    settle(0)
     for cp in stores:
         cp.wait()
     for cp in started:
@@ -422,6 +416,8 @@
     for k in range(2):
         gather_close(k)
         share_close(k)
+        for level in range(levels):
+            gossip_copy(k, level).wait_send()
 
 
 def copy_kernel(gi, nw, nm, gi_out, nw_out, nm_out, gi_at, w_at, m_at, came, left):
@@ -470,9 +466,8 @@
             vm((3, ext * cols, chans), BF16),
             vm((3, ext * cols, chans), BF16),
             vm((3, ext * cols, chans), BF16),
-            vm((3 * chans, rows * cols), BF16),
-            vm((3 * chans, ext * cols), BF16),
-            vm((rows * cols, chans), BF16),
+            vm((chans, ext * cols), BF16),
+            vm((chans, rows * cols), BF16),
             vm((rows * cols, chans), F32),
             vm((rows * cols, chans), BF16),
             vm((2, kc, chans), BF16),
@@ -504,7 +499,7 @@
         out_specs=(any_space,) * 3,
         scratch_shapes=[vm(gi.shape, BF16), vm(nw.shape, F32), vm(nm.shape, F32),
                         sem((rows + 4,)), sem((rows + 4,))],
-        compiler_params=pltpu.CompilerParams(vmem_limit_bytes=16 * 1024 * 1024),
+        compiler_params=pltpu.CompilerParams(vmem_limit_bytes=63 * 1024 * 1024),
     )(gi, nw, nm)
     return gi[None], nw[None], nm[None]
 

time: 92.6 us -> 87.8 us (0.948)
  local copies, waits for them, and re-layouts: 3.71 us -> 0 us
    unnamed x6 -> x0, local copies, waits for them, and re-layouts: 3.71 us -> none
    pallas_call x1, Pallas kernels: 84.3 us -> 82.9 us  [shards(): pl.pallas_call(partial(block_kernel, n, reps, levels, scale), out_shape=(...]
where the time goes in v3:
time: 87.8 us; the launch traced here: 87.6 us
  Pallas kernels  85.8 us (98%)
  between operations  1.3 us (1%)
    pallas_call x1, Pallas kernels, shards(): pl.pallas_call(partial(block_kernel, n, reps, levels, scale), out_shape=(...  82.9 us
    pallas_call x1, Pallas kernels, shards(): pl.pallas_call(copy_kernel, out_shape=tuple((jax.ShapeDtypeStruct(v.shape...  2.85 us

profile of v3, /device:TPU:8, one launch (start us, length us, event | category | flops | bytes accessed | tf_op | source)
XLA Modules:
  0.0 87.6 jit_solution(4084302216141305507)
XLA Ops:
  1.3 0.5 compare_convert_fusion.coef
  1.8 82.9 %shard_map.85 = (bf16[8,512,256]{2,1,0:T(8,128)(2,1)}, f32[2,288,256]{2,1,0:T(8,128)}, f32[2,288,256]{2,1,0:T(8,128)}) custom-call(f32[2]{0:T(128)} %compare_convert_fusion.coef, bf16[8,512,256]{2,1,0:T(8,128)(2,1)} %bitcast.11, bf16[8,512,256]{2,1,0:T(8,128)(2,1)} %bitcast.12, s32[8,512]{1,0:T(8,128)} %mask_ref.1, f32[2,288,256]{2,1,0:T(8,128)} %bitcast.14, ...), custom_call_target="tpu_custom_call" | custom-call | flops 24159191040 | bytes 12582912 | tf_op jit(solution)/shard_map/pallas_call | solution.py:455
  84.8 2.9 %shard_map.86 = (bf16[8,512,256]{2,1,0:T(8,128)(2,1)}, f32[2,288,256]{2,1,0:T(8,128)}, f32[2,288,256]{2,1,0:T(8,128)}) custom-call(bf16[8,512,256]{2,1,0:T(8,128)(2,1)} %get-tuple-element.9.gi, f32[2,288,256]{2,1,0:T(8,128)} %get-tuple-element.10.nw, f32[2,288,256]{2,1,0:T(8,128)} %get-tuple-element.11.nm), custom_call_target="tpu_custom_call" | custom-call | tf_op jit(solution)/shard_map/pallas_call | solution.py:495

commit v4 on v3

--- a/solution.py
+++ b/solution.py
@@ -188,6 +188,74 @@
         v = cot[pl.ds(r * cols, cols), :].astype(F32) * mask_t[:, r:r + 1]
         ms[1, pl.ds((r + 1) * cols, cols), :] = v.astype(BF16)
 
+    for r in order:
+        mask_row(r)
+    gather_hop(0, 1)
+    for r in order:
+        x_in[r].wait()
+
+    def prep_x(r):
+        v = xs[1, span(r), :]
+        x_t[:, span(r)] = jnp.transpose(v)
+        sides(xs, r, v.astype(F32))
+
+    def prep_m(r):
+        sides(ms, r, ms[1, span(r), :].astype(F32))
+
+    def edges(prep):
+        @pl.loop(0, 2)
+        def _(e):
+            prep(e * (ext - 1))
+
+    @pl.loop(1, rows + 1)
+    def _(r):
+        prep_x(r)
+
+    if nz > 2:
+        gather_hop(0, 2)
+
+    @pl.loop(1, rows + 1)
+    def _(r):
+        prep_m(r)
+
+    for hop in range(3, nz):
+        gather_hop(0, hop)
+    halo(0, xs, True)
+    halo(1, ms, True)
+    gather_start(1)
+    gather_finish(0)
+
+    def conv(buf, ker, h, ahead, count=2):
+        parts = []
+        for i in range(3):
+            for j in range(3):
+                a, b = (i, j) if ahead else (2 - i, 2 - j)
+                parts.append(buf[b, span(h + a, count), :])
+        return jnp.dot(jnp.concatenate(parts, axis=1), ker[...], preferred_element_type=F32)
+
+    def turn(k):
+        @pl.loop(0, taps)
+        def _(t):
+            at = pl.ds(pl.multiple_of(t * chans, chans), chans)
+            k_t[k, at, :] = jnp.transpose(kf[k, at, :])
+
+    half = rows // 2
+
+    @pl.loop(0, half)
+    def _(e):
+        @pl.when(e == half - 2)
+        def _():
+            gather_hop(1, 1)
+            halo(0, xs, False)
+            edges(prep_x)
+
+        h = (2 * e + 2) % rows
+        for r in (h, h + 1):
+            pre = conv(xs, kf.at[0], r, True, 1)
+            sig = 0.5 * jnp.tanh(0.5 * pre) + 0.5
+            slope[span(r), :] = sig * (1.0 + pre * (1.0 - sig))
+            h_t[:, span(r)] = jnp.transpose((pre * sig).astype(BF16))
+
     mb[...] = mom_ref[...].astype(BF16)
     for level in range(levels):
         to = (q + (1 << level)) % reps
@@ -196,73 +264,6 @@
             cp.start()
             started.append(cp)
     early = started[-2 * levels:]
-
-    for r in order:
-        mask_row(r)
-    gather_hop(0, 1)
-    for r in order:
-        x_in[r].wait()
-
-    def prep_x(r):
-        v = xs[1, span(r), :]
-        x_t[:, span(r)] = jnp.transpose(v)
-        sides(xs, r, v.astype(F32))
-
-    def prep_m(r):
-        sides(ms, r, ms[1, span(r), :].astype(F32))
-
-    def edges(prep):
-        @pl.loop(0, 2)
-        def _(e):
-            prep(e * (ext - 1))
-
-    @pl.loop(1, rows + 1)
-    def _(r):
-        prep_x(r)
-
-    if nz > 2:
-        gather_hop(0, 2)
-
-    @pl.loop(1, rows + 1)
-    def _(r):
-        prep_m(r)
-
-    for hop in range(3, nz):
-        gather_hop(0, hop)
-    halo(0, xs, True)
-    halo(1, ms, True)
-    gather_start(1)
-    gather_finish(0)
-
-    def conv(buf, ker, h, ahead):
-        parts = []
-        for i in range(3):
-            for j in range(3):
-                a, b = (i, j) if ahead else (2 - i, 2 - j)
-                parts.append(buf[b, span(h + a, 2), :])
-        return jnp.dot(jnp.concatenate(parts, axis=1), ker[...], preferred_element_type=F32)
-
-    def turn(k):
-        @pl.loop(0, taps)
-        def _(t):
-            at = pl.ds(pl.multiple_of(t * chans, chans), chans)
-            k_t[k, at, :] = jnp.transpose(kf[k, at, :])
-
-    half = rows // 2
-
-    @pl.loop(0, half)
-    def _(e):
-        @pl.when(e == half - 2)
-        def _():
-            gather_hop(1, 1)
-            halo(0, xs, False)
-            edges(prep_x)
-
-        h = (2 * e + 2) % rows
-        pre = conv(xs, kf.at[0], h, True)
-        sig = 0.5 * jnp.tanh(0.5 * pre) + 0.5
-        slope[span(h, 2), :] = sig * (1.0 + pre * (1.0 - sig))
-        h_t[:, span(h, 2)] = jnp.transpose((pre * sig).astype(BF16))
 
     if nz > 2:
         gather_hop(1, 2)
@@ -349,10 +350,10 @@
     @pl.loop(0, half)
     def _(e):
         h = (2 * e + rows - 2) % rows
-        v = conv(ms, k_t.at[1], h, False) * slope[span(h, 2), :]
-        ps[1, span(h + 1, 2), :] = v.astype(BF16)
-        sides(ps, h + 1, v[:cols])
-        sides(ps, h + 2, v[cols:])
+        for r in (h, h + 1):
+            v = conv(ms, k_t.at[1], r, False, 1) * slope[span(r), :]
+            ps[1, span(r + 1), :] = v.astype(BF16)
+            sides(ps, r + 1, v)
 
         @pl.when(e == 1)
         def _():

time: 87.8 us -> 88.1 us (level)
  no operation moved by 1% of the time
where the time goes in v4:
time: 88.1 us; the launch traced here: 88 us
  Pallas kernels  86.1 us (98%)
  between operations  1.3 us (1%)
    pallas_call x1, Pallas kernels, shards(): pl.pallas_call(partial(block_kernel, n, reps, levels, scale), out_shape=(...  83.3 us
    pallas_call x1, Pallas kernels, shards(): pl.pallas_call(copy_kernel, out_shape=tuple((jax.ShapeDtypeStruct(v.shape...  2.85 us

profile of v4, /device:TPU:8, one launch (start us, length us, event | category | flops | bytes accessed | tf_op | source)
XLA Modules:
  0.0 88.0 jit_solution(6123085847362820963)
XLA Ops:
  1.3 0.5 compare_convert_fusion.coef
  1.8 83.3 %shard_map.85 = (bf16[8,512,256]{2,1,0:T(8,128)(2,1)}, f32[2,288,256]{2,1,0:T(8,128)}, f32[2,288,256]{2,1,0:T(8,128)}) custom-call(f32[2]{0:T(128)} %compare_convert_fusion.coef, bf16[8,512,256]{2,1,0:T(8,128)(2,1)} %bitcast.11, bf16[8,512,256]{2,1,0:T(8,128)(2,1)} %bitcast.12, s32[8,512]{1,0:T(8,128)} %mask_ref.1, f32[2,288,256]{2,1,0:T(8,128)} %bitcast.14, ...), custom_call_target="tpu_custom_call" | custom-call | flops 24159191040 | bytes 12582912 | tf_op jit(solution)/shard_map/pallas_call | solution.py:456
  85.1 2.9 %shard_map.86 = (bf16[8,512,256]{2,1,0:T(8,128)(2,1)}, f32[2,288,256]{2,1,0:T(8,128)}, f32[2,288,256]{2,1,0:T(8,128)}) custom-call(bf16[8,512,256]{2,1,0:T(8,128)(2,1)} %get-tuple-element.9.gi, f32[2,288,256]{2,1,0:T(8,128)} %get-tuple-element.10.nw, f32[2,288,256]{2,1,0:T(8,128)} %get-tuple-element.11.nm), custom_call_target="tpu_custom_call" | custom-call | tf_op jit(solution)/shard_map/pallas_call | solution.py:496
